TPU v7x, 512 devices: a whole 4x4x16 slice. The times are simulated.
512 devices in a mesh: brick: 128 (over y, z_hi, x, core), plane: 4 (over z_lo).
Axes of the slice: x: 4, y: 4, z: 16 (z_hi: 4, z_lo: 4; z = z_hi * 4 + z_lo), core: 2. Of those that a mesh axis runs over, the one named last changes fastest.
Arguments:
- positions: float32 [128, 4, 3, 4096], P('brick', 'plane'), may hold values from 0 to 64
- aux: float32 [128, 4, 4096], P('brick', 'plane'), may hold values from -1 to 1.8
- aux_prev: float32 [128, 4, 4096], P('brick', 'plane'), may hold values from -3 to 3
- resid: float32 [128, 4, 4096], P('brick', 'plane'), may hold values from -2 to 2
- types: int32 [128, 4, 4096], P('brick', 'plane'), may hold values from 0 to 7
- pair_tiles: int32 [128, 4, 1496], P('brick', 'plane'), may hold values from 0 to 63, as said below
- pair_cands: int32 [128, 4, 1496], P('brick', 'plane'), may hold values from 0 to 319, as said below
- pair_count: int32 [128, 4], P('brick', 'plane'), may hold values from 0 to 1496, as said below
- owner_tile: int32 [128, 4, 64], P('brick', 'plane'), may hold values from 0 to 255, as said below
- electroneg: float32 [8], replicated, may hold values from -3 to 3
- hardness: float32 [8], replicated, may hold values from 6 to 14
- widths: float32 [8], replicated, may hold values from 0.6 to 2
Outputs:
- charges: float32 [128, 4, 4096], P('brick', 'plane')
- next_aux: float32 [128, 4, 4096], P('brick', 'plane')
- resid_field: float32 [128, 4, 4096], P('brick', 'plane')
Inputs may be any that keep to these rules, and one draw needn't show every extreme that they name: `pair_tiles`: entries after the first pair_count[b, p] of a brick's list are not used. `pair_cands`: A used pair never names a neighbour brick beyond the ends of the brick axis. `pair_count`: at most 1496 pairs a brick, reached by some brick. `owner_tile`: for each b the values over all p and t form a permutation of 0 to 255, and each brick (b, p) has exactly 16 tiles of each value // 64.
All inputs are finite; a program needn't handle non-finite values.
Results may differ from a plain program's by a relative error of at most 0.0003.
Values sent between devices are 32-bit elements; how exact they have to be, the bound alone decides.
A program may use at most 64 MiB of HBM per device.

v0:
```python
import jax
import jax.numpy as jnp
from jax import lax
from jax.sharding import PartitionSpec as P

TX = 2
TY = 4
TILE = 64
cell_edge = 8.0
cutoff = 10.0
soften = 0.5
kappa = 1.86
pair_group = 256


def extended(block, sides, width):
    for axis, dim in sides:
        count = lax.axis_size(axis)
        forward = [(i, i + 1) for i in range(count - 1)]
        forward.append((count - 1, 0))
        backward = [(target, source) for source, target in forward]
        low = lax.ppermute(
            lax.slice_in_dim(block, block.shape[dim] - width, None, axis=dim), axis, forward
        )
        high = lax.ppermute(lax.slice_in_dim(block, 0, width, axis=dim), axis, backward)
        block = jnp.concatenate([low, block, high], axis=dim)
    return block


def lookup(type_table, type_row):
    chosen = (
        type_row[None, :] == jnp.arange(type_table.shape[0], dtype=jnp.int32)[:, None]
    ).astype(type_table.dtype)
    return jnp.sum(type_table[:, None] * chosen, axis=0)


def candidates(blocks, tile_count):
    joined = jnp.stack(blocks, axis=1)
    offsets = jnp.zeros((6, 5), jnp.float32)
    offsets = offsets.at[0, 1].set(-TX * cell_edge).at[0, 2].set(TX * cell_edge)
    offsets = offsets.at[1, 3].set(-TY * cell_edge).at[1, 4].set(TY * cell_edge)
    joined = joined + offsets[:, :, None]
    return joined.reshape(6, 5 * tile_count, TILE)


def pair_terms(home_tiles, candidate, near_ids, far_ids, in_range):
    tile_count = home_tiles.shape[1]
    near_atoms = jnp.take(home_tiles, near_ids, axis=1)
    far_atoms = jnp.take(candidate, far_ids, axis=1)
    delta_x = near_atoms[0][:, :, None] - far_atoms[0][:, None, :]
    delta_y = near_atoms[1][:, :, None] - far_atoms[1][:, None, :]
    delta_z = near_atoms[2][:, :, None] - far_atoms[2][:, None, :]
    dist_sq = delta_x * delta_x + delta_y * delta_y + delta_z * delta_z
    spacing = jnp.sqrt(dist_sq + soften * soften)
    inv_width = lax.rsqrt(near_atoms[5][:, :, None] ** 2 + far_atoms[5][:, None, :] ** 2)
    taper = jnp.square(jnp.maximum(1.0 - dist_sq / (cutoff * cutoff), 0.0))
    kernel = jax.scipy.special.erf(inv_width * spacing) / spacing * taper
    diagonal = (
        jnp.arange(TILE, dtype=jnp.int32)[:, None] == jnp.arange(TILE, dtype=jnp.int32)[None, :]
    )
    self_pairs = (far_ids == near_ids)[:, None, None] & diagonal[None]
    kept_pairs = in_range[:, None, None] & jnp.logical_not(self_pairs)
    kernel = jnp.where(kept_pairs, kernel, 0.0)
    pair_fields = jnp.einsum(
        "pij,cpj->cpi", kernel, far_atoms[3:5], precision=lax.Precision.HIGHEST
    )
    chosen = (near_ids[:, None] == jnp.arange(tile_count, dtype=jnp.int32)[None, :]).astype(
        pair_fields.dtype
    )
    return jnp.einsum("pt,cpi->cti", chosen, pair_fields, precision=lax.Precision.HIGHEST)


def sweep(home_tiles, candidate, near_list, far_list, begin_pair, end_pair, running):
    near_pad = jnp.concatenate([near_list, jnp.zeros((pair_group,), jnp.int32)])
    far_pad = jnp.concatenate([far_list, jnp.zeros((pair_group,), jnp.int32)])
    turns = (end_pair - begin_pair + pair_group - 1) // pair_group

    def advance(block_index, running):
        offset_start = begin_pair + block_index * pair_group
        near_ids = lax.dynamic_slice_in_dim(near_pad, offset_start, pair_group)
        far_ids = lax.dynamic_slice_in_dim(far_pad, offset_start, pair_group)
        in_range = offset_start + jnp.arange(pair_group, dtype=jnp.int32) < end_pair
        return running + pair_terms(home_tiles, candidate, near_ids, far_ids, in_range)

    return lax.fori_loop(0, turns, advance, running)


def on_device(
    positions,
    aux,
    aux_prev,
    resid,
    types,
    pair_tiles,
    pair_cands,
    pair_count,
    owner_tile,
    electroneg,
    hardness,
    widths,
):
    atom_count = aux.shape[-1]
    tile_count = atom_count // TILE
    type_row = types.reshape(atom_count)
    negativity = lookup(electroneg, type_row)
    hardness_row = lookup(hardness, type_row)
    radius = lookup(widths, type_row)
    charge_row = aux.reshape(atom_count)
    resid_row = resid.reshape(atom_count)
    packed = jnp.concatenate(
        [positions.reshape(3, atom_count), charge_row[None], resid_row[None], radius[None]], axis=0
    )
    rimmed = extended(packed[None, None], (("brick", 0), ("plane", 1)), 1)
    candidate = candidates(
        [rimmed[1, 1], rimmed[0, 1], rimmed[2, 1], rimmed[1, 0], rimmed[1, 2]], tile_count
    )
    home_tiles = packed.reshape(6, tile_count, TILE)
    near_list = pair_tiles.reshape(-1)
    far_list = pair_cands.reshape(-1)
    pair_total = pair_count.reshape(())
    start_total = jnp.zeros((2, tile_count, TILE), jnp.float32)
    totals = sweep(home_tiles, candidate, near_list, far_list, 0, pair_total, start_total)
    aux_field = totals[0].reshape(atom_count)
    resid_field = totals[1].reshape(atom_count)
    field = negativity + aux_field + resid_field
    global_sums = lax.psum(
        (jnp.sum(charge_row), jnp.sum(field / hardness_row), jnp.sum(1.0 / hardness_row)),
        ("brick", "plane"),
    )
    potential_level = (global_sums[0] + global_sums[1]) / global_sums[2]
    charges = (potential_level - field) / hardness_row
    stacked = jnp.stack([charge_row, charges]).reshape(2, tile_count, TILE)
    target = owner_tile.reshape(tile_count)
    planes = lax.axis_size("plane")
    gathered, gathered_slots = (
        lax.all_gather(stacked[None], "plane", axis=0, tiled=True),
        lax.all_gather(target.astype(jnp.float32)[None], "plane", axis=0, tiled=True),
    )
    whole = jnp.transpose(gathered, (1, 0, 2, 3)).reshape(2, planes * tile_count, TILE)
    slot_ids = gathered_slots.reshape(planes * tile_count).astype(jnp.int32)
    mine = lax.axis_index("plane") * tile_count + jnp.arange(tile_count, dtype=jnp.int32)
    placer = (slot_ids[None, :] == mine[:, None]).astype(jnp.float32)
    placed = jnp.einsum("sk,ckj->csj", placer, whole, precision=lax.Precision.HIGHEST)
    previous = aux_prev.reshape(tile_count, TILE)
    next_aux = 2.0 * placed[0] - previous + kappa * (placed[1] - placed[0])
    return (charges.reshape(aux.shape), next_aux.reshape(aux.shape), resid_field.reshape(aux.shape))


def solution(mesh):
    in_specs = (
        P("brick", "plane", None, None),
        P("brick", "plane", None),
        P("brick", "plane", None),
        P("brick", "plane", None),
        P("brick", "plane", None),
        P("brick", "plane", None),
        P("brick", "plane", None),
        P("brick", "plane"),
        P("brick", "plane", None),
        P(),
        P(),
        P(),
    )
    out_specs = (P("brick", "plane", None), P("brick", "plane", None), P("brick", "plane", None))
    return jax.shard_map(
        on_device, mesh=mesh, in_specs=in_specs, out_specs=out_specs, check_vma=False
    )
```

profile of v0, /device:TPU:32, one launch (start us, length us, event | category | flops | bytes accessed | tf_op | source)
XLA Modules:
  0.0 361.1 jit_solution(17657428867566629338)
XLA Ops:
  0.7 0.8 copy.57
  1.5 0.9 select_reduce_fusion.2
  2.4 0.8 fusion.37
  3.2 1.9 collective-permute-start
  5.2 15.9 %collective-permute-start.1 = (f32[1,1,6,4096]{3,2,1,0:T(8,128)S(1)}, f32[1,1,6,4096]{3,2,1,0:T(8,128)S(1)}, u32[]{:S(2)}, u32[]{:S(2)}) collective-permute-start(f32[1,1,6,4096]{3,2,1,0:T(8,128)S(1)} %fusion.37), channel_id=1, source_target_pairs={{4,0},{8,4},{12,8},{16,12},{20,16},{24,20},{28,24},{32,28},{36,32}... | collective-permute-start | bytes 294920 | tf_op jit(solution)/shard_map/ppermute | solution.py:25
  21.1 0.8 bitcast_dynamic-update-slice_fusion.2
  22.6 0.5 broadcast.209
  23.1 2.1 fusion.46
  25.2 1.4 reduce.31
  26.6 0.9 reduce.17
  27.6 0.6 divide_reduce_fusion
  28.5 0.6 fusion.48
  29.1 0.6 fusion.47
  29.7 1.3 and_reduce_fusion
  31.0 1.4 scatter.14
  32.4 1.9 dynamic-slice.29
  35.5 1.4 scatter.15
  38.0 9.1 %all-gather = f32[4,1,64]{2,1,0:T(1,128)S(1)} all-gather(f32[1,1,64]{2,1,0:T(1,128)S(1)} %convert_element_type.28), channel_id=2, replica_groups=mesh['brick'=128,'plane'=4] {'plane'}, dimensions={0}, use_global_device_ids=true | all-gather | bytes 1280 | tf_op jit(solution)/shard_map/all_gather | solution.py:137
  47.2 1.9 collective-permute-start.2
  49.1 3.9 %collective-permute-start.3 = (f32[3,1,6,4096]{3,2,1,0:T(8,128)S(1)}, f32[3,1,6,4096]{3,2,1,0:T(8,128)S(1)}, u32[]{:S(2)}, u32[]{:S(2)}) collective-permute-start(f32[3,1,6,4096]{3,2,1,0:T(8,128)S(1)} %pad_maximum_fusion), channel_id=1, source_target_pairs={{1,0},{2,1},{3,2},{0,3},{5,4},{6,5},{7,6},{4,7},{9,8},{10,9},{11,1... | collective-permute-start | bytes 884744 | tf_op jit(solution)/shard_map/ppermute | solution.py:25
  53.1 3.8 %collective-permute-done.2 = f32[3,1,6,4096]{3,2,1,0:T(8,128)S(1)} collective-permute-done((f32[3,1,6,4096]{3,2,1,0:T(8,128)S(1)}, f32[3,1,6,4096]{3,2,1,0:T(8,128)S(1)}, u32[]{:S(2)}, u32[]{:S(2)}) %collective-permute-start.2) | collective-permute-done | bytes 294944 | tf_op jit(solution)/shard_map/ppermute | solution.py:22
  56.9 6.0 %collective-permute-done.3 = f32[3,1,6,4096]{3,2,1,0:T(8,128)S(1)} collective-permute-done((f32[3,1,6,4096]{3,2,1,0:T(8,128)S(1)}, f32[3,1,6,4096]{3,2,1,0:T(8,128)S(1)}, u32[]{:S(2)}, u32[]{:S(2)}) %collective-permute-start.3) | collective-permute-done | bytes 294944 | tf_op jit(solution)/shard_map/ppermute | solution.py:25
  63.2 0.4 stack.12
  63.9 0.6 copy.46
  64.5 57.3 %while.14 = (s32[]{:T(128)}, f32[2,64,64]{1,2,0:T(8,128)S(1)}, s32[]{:T(128)}, s32[1752]{0:T(1024)S(1)}, f32[6,320,64]{2,0,1:T(8,128)S(1)}, /*index=5*/s32[]{:T(...) while((s32[]{:T(128)}, f32[2,64,64]{1,2,0:T(8,128)S(1)}, ...), condition=%wide.region_6.0_spmd, body=%wide.region_5.0_spmd.sunk | while | flops 72616448 | bytes 5868207 | solution.py:85
  64.6 0.7 dynamic-slice_compare_fusion.2
  65.3 1.0 gather_fusion.1
  66.4 0.3 select_bitcast_fusion.5
  66.7 0.4 slice_multiply_fusion.6
  67.1 1.0 gather_fusion
  68.1 0.3 select_bitcast_fusion.4
  68.5 0.4 slice_multiply_fusion.5
  68.9 23.9 %fusion.66 = f32[2,256,64]{2,0,1:T(2,128)S(1)} fusion(f32[256,64]{1,0:T(8,128)S(1)} %bitcast.106, f32[256,64]{1,0:T(8,128)S(1)} %bitcast.102, f32[256,64]{1,0:T(8,128)S(1)} %bitcast.107, f32[256,64]{1,0:T(8,128)S(1)} %bitcast.103, f32[256,64]{1,0:T(8,128)S(1)} %bitcast.108, f32[256,64]{1,0:T(8,128)S(1)} %bitcast.104, f32[256,64]{1,0:T(8,128)S(1)} %bitcast.105, ...), kind=kOutput, calls=%fused_computation.24.clone.3 | convolution fusion | flops 47185920 | bytes 1451008 | tf_op jit(solution)/shard_map/while/body/pij,cpj->cpi/dot_general | solution.py:64
  92.8 0.4 fusion.67
  93.2 0.7 dynamic-slice_compare_fusion.2
  94.0 1.0 gather_fusion.1
  95.0 0.3 select_bitcast_fusion.5
  95.4 0.4 slice_multiply_fusion.6
  95.8 1.0 gather_fusion
  96.8 0.3 select_bitcast_fusion.4
  97.2 0.4 slice_multiply_fusion.5
  97.6 23.9 %fusion.66 = f32[2,256,64]{2,0,1:T(2,128)S(1)} fusion(f32[256,64]{1,0:T(8,128)S(1)} %bitcast.106, f32[256,64]{1,0:T(8,128)S(1)} %bitcast.102, f32[256,64]{1,0:T(8,128)S(1)} %bitcast.107, f32[256,64]{1,0:T(8,128)S(1)} %bitcast.103, f32[256,64]{1,0:T(8,128)S(1)} %bitcast.108, f32[256,64]{1,0:T(8,128)S(1)} %bitcast.104, f32[256,64]{1,0:T(8,128)S(1)} %bitcast.105, ...), kind=kOutput, calls=%fused_computation.24.clone.3 | convolution fusion | flops 47185920 | bytes 1451008 | tf_op jit(solution)/shard_map/while/body/pij,cpj->cpi/dot_general | solution.py:64
  121.5 0.4 fusion.67
  122.0 0.6 fusion.44
  124.0 218.8 %all-reduce.2 = (f32[]{:T(128)}, f32[]{:T(128)}) all-reduce(f32[]{:T(128)S(6)} %add.163, f32[]{:T(128)} %divide_reduce_fusion), channel_id=1, replica_groups=mesh['brick'=128,'plane'=4] {'brick','plane'}, use_global_device_ids=true, to_apply=%region_1.0 | all-reduce | flops 2 | bytes 16 | tf_op jit(solution)/shard_map/psum | solution.py:126
  344.2 14.4 %all_gather.6 = f32[4,2,64,64]{3,2,1,0:T(8,128)S(1)} all-gather(f32[1,2,64,64]{3,2,1,0:T(8,128)S(1)} %pad_maximum_fusion.3), channel_id=1, replica_groups=mesh['brick'=128,'plane'=4] {'plane'}, dimensions={0}, use_global_device_ids=true | all-gather | bytes 163840 | tf_op jit(solution)/shard_map/all_gather | solution.py:136
  359.8 0.6 subtract_add_fusion
  360.5 0.6 subtract_divide_fusion
  (71 shorter events, 3.5 us)
Async XLA Ops:
  0.6 37.3 %copy-start = (f32[1,1,4096]{2,1,0:T(1,128)S(1)}, f32[1,1,4096]{2,1,0:T(1,128)}, u32[]{:S(2)}) copy-start(f32[1,1,4096]{2,1,0:T(1,128)} %param.23) | copy-start | bytes 49156
  0.6 37.2 %copy-start.3 = (s32[1,1,1496]{2,1,0:T(1,128)S(1)}, s32[1,1,1496]{2,1,0:T(1,128)}, u32[]{:S(2)}) copy-start(s32[1,1,1496]{2,1,0:T(1,128)} %param.28) | copy-start | bytes 17956
  0.7 37.2 %copy-start.4 = (s32[1,1,1496]{2,1,0:T(1,128)S(1)}, s32[1,1,1496]{2,1,0:T(1,128)}, u32[]{:S(2)}) copy-start(s32[1,1,1496]{2,1,0:T(1,128)} %param.27) | copy-start | bytes 17956
  0.7 37.3 %copy-start.5 = (s32[1,1,64]{2,1,0:T(1,128)S(1)}, s32[1,1,64]{2,1,0:T(1,128)}, u32[]{:S(2)}) copy-start(s32[1,1,64]{2,1,0:T(1,128)} %param.30) | copy-start | bytes 772
  3.2 43.9 %collective-permute-start = (f32[1,1,6,4096]{3,2,1,0:T(8,128)S(1)}, f32[1,1,6,4096]{3,2,1,0:T(8,128)S(1)}, u32[]{:S(2)}, u32[]{:S(2)}) collective-permute-start(f32[1,1,6,4096]{3,2,1,0:T(8,128)S(1)} %fusion.37), channel_id=1, source_target_pairs={{0,4},{4,8},{8,12},{12,16},{16,20},{20,24},{24,28},{28,32},{32,36}... | collective-permute-start | bytes 294920 | tf_op jit(solution)/shard_map/ppermute | solution.py:22
  5.2 42.0 %collective-permute-start.1 = (f32[1,1,6,4096]{3,2,1,0:T(8,128)S(1)}, f32[1,1,6,4096]{3,2,1,0:T(8,128)S(1)}, u32[]{:S(2)}, u32[]{:S(2)}) collective-permute-start(f32[1,1,6,4096]{3,2,1,0:T(8,128)S(1)} %fusion.37), channel_id=1, source_target_pairs={{4,0},{8,4},{12,8},{16,12},{20,16},{24,20},{28,24},{32,28},{36,32}... | collective-permute-start | bytes 294920 | tf_op jit(solution)/shard_map/ppermute | solution.py:25
  47.2 9.7 %collective-permute-start.2 = (f32[3,1,6,4096]{3,2,1,0:T(8,128)S(1)}, f32[3,1,6,4096]{3,2,1,0:T(8,128)S(1)}, u32[]{:S(2)}, u32[]{:S(2)}) collective-permute-start(f32[3,1,6,4096]{3,2,1,0:T(8,128)S(1)} %pad_maximum_fusion), channel_id=1, source_target_pairs={{0,1},{1,2},{2,3},{3,0},{4,5},{5,6},{6,7},{7,4},{8,9},{9,10},{10,1... | collective-permute-start | bytes 884744 | tf_op jit(solution)/shard_map/ppermute | solution.py:22
  49.1 13.8 %collective-permute-start.3 = (f32[3,1,6,4096]{3,2,1,0:T(8,128)S(1)}, f32[3,1,6,4096]{3,2,1,0:T(8,128)S(1)}, u32[]{:S(2)}, u32[]{:S(2)}) collective-permute-start(f32[3,1,6,4096]{3,2,1,0:T(8,128)S(1)} %pad_maximum_fusion), channel_id=1, source_target_pairs={{1,0},{2,1},{3,2},{0,3},{5,4},{6,5},{7,6},{4,7},{9,8},{10,9},{11,1... | collective-permute-start | bytes 884744 | tf_op jit(solution)/shard_map/ppermute | solution.py:25
  121.9 237.9 %copy-start.2 = (f32[1,1,4096]{2,1,0:T(1,128)S(1)}, f32[1,1,4096]{2,1,0:T(1,128)}, u32[]{:S(2)}) copy-start(f32[1,1,4096]{2,1,0:T(1,128)} %param.24) | copy-start | bytes 49156
  359.8 1.3 copy-start.1
where the time goes:
time: 362 us; the launch traced here: 361 us
  blocking collectives  242 us (67%)
  matrix products  48.9 us (14%)
  starting transfers between devices  23.7 us (7%)
  other arithmetic  15.6 us (4%)
  local copies, waits for them, and re-layouts  15 us (4%)
  waiting for transfers between devices  9.81 us (3%)
  between operations  5.63 us (2%)
    psum x1, blocking collectives, on_device(): lax.psum((jnp.sum(charge_row), jnp.sum(field / hardness_row), jnp.sum(1.0...  219 us
    dot_general x2, matrix products, pair_terms(): jnp.einsum('pij,cpj->cpi', kernel, far_atoms[3:5], precision=lax.Precisio...  47.9 us
    ppermute x2, starting transfers between devices, extended(): lax.ppermute(lax.slice_in_dim(block, 0, width, axis=dim), axis, backward)  19.8 us
    all_gather x1, blocking collectives, on_device(): lax.all_gather(stacked[None], 'plane', axis=0, tiled=True)  14.4 us
    all_gather x1, blocking collectives, on_device(): lax.all_gather(target.astype(jnp.float32)[None], 'plane', axis=0, tiled=T...  9.07 us
  transfers between devices with their start and end apart: 4, of which 2 were waited for; matrix products, arithmetic and copies ran while one was open for 4% of the time, Pallas kernels for 0%

commit v1 on v0

--- a/solution.py
+++ b/solution.py
@@ -124,8 +124,11 @@
     resid_field = totals[1].reshape(atom_count)
     field = negativity + aux_field + resid_field
     global_sums = lax.psum(
-        (jnp.sum(charge_row), jnp.sum(field / hardness_row), jnp.sum(1.0 / hardness_row)),
-        ("brick", "plane"),
+        lax.psum(
+            (jnp.sum(charge_row), jnp.sum(field / hardness_row), jnp.sum(1.0 / hardness_row)),
+            "brick",
+        ),
+        "plane",
     )
     potential_level = (global_sums[0] + global_sums[1]) / global_sums[2]
     charges = (potential_level - field) / hardness_row

time: 362 us -> 664 us (1.83)
  blocking collectives: 242 us -> 545 us
    psum x1, blocking collectives: 219 us -> 512 us  [on_device(): lax.psum((jnp.sum(charge_row), jnp.sum(field / hardness_row), jnp.sum(1.0...]
    psum x0 -> x1, blocking collectives: none -> 11.1 us  [on_device(): lax.psum(lax.psum((jnp.sum(charge_row), jnp.sum(field / hardness_row), jn...]
  transfers between devices with their start and end apart: 4 -> 4, of which waited for: 2 -> 2; matrix products, arithmetic and copies ran while one was open for 4% -> 2% of each run, Pallas kernels for 0% -> 0%
where the time goes in v1:
time: 664 us; the launch traced here: 663 us
  blocking collectives  545 us (82%)
  matrix products  48.9 us (7%)
  starting transfers between devices  23.7 us (4%)
  other arithmetic  15.6 us (2%)
  local copies, waits for them, and re-layouts  15 us (2%)
  waiting for transfers between devices  9.81 us (1%)
    psum x1, blocking collectives, on_device(): lax.psum((jnp.sum(charge_row), jnp.sum(field / hardness_row), jnp.sum(1.0...  512 us
    dot_general x2, matrix products, pair_terms(): jnp.einsum('pij,cpj->cpi', kernel, far_atoms[3:5], precision=lax.Precisio...  47.9 us
    ppermute x2, starting transfers between devices, extended(): lax.ppermute(lax.slice_in_dim(block, 0, width, axis=dim), axis, backward)  19.8 us
  transfers between devices with their start and end apart: 4, of which 2 were waited for; matrix products, arithmetic and copies ran while one was open for 2% of the time, Pallas kernels for 0%

profile of v1, /device:TPU:32, one launch (start us, length us, event | category | flops | bytes accessed | tf_op | source)
XLA Modules:
  0.0 663.4 jit_solution(11263928648147417900)
XLA Ops:
  0.7 0.8 copy.57
  1.5 0.9 select_reduce_fusion.2
  2.4 0.8 fusion.37
  3.2 1.9 collective-permute-start
  5.2 15.9 %collective-permute-start.1 = (f32[1,1,6,4096]{3,2,1,0:T(8,128)S(1)}, f32[1,1,6,4096]{3,2,1,0:T(8,128)S(1)}, u32[]{:S(2)}, u32[]{:S(2)}) collective-permute-start(f32[1,1,6,4096]{3,2,1,0:T(8,128)S(1)} %fusion.37), channel_id=1, source_target_pairs={{4,0},{8,4},{12,8},{16,12},{20,16},{24,20},{28,24},{32,28},{36,32}... | collective-permute-start | bytes 294920 | tf_op jit(solution)/shard_map/ppermute | solution.py:25
  21.1 0.8 bitcast_dynamic-update-slice_fusion.2
  22.6 0.5 broadcast.209
  23.1 2.1 fusion.46
  25.2 1.4 reduce.31
  26.6 0.9 reduce.17
  27.6 0.6 divide_reduce_fusion
  28.5 0.6 fusion.48
  29.1 0.6 fusion.47
  29.7 1.3 and_reduce_fusion
  31.0 1.4 scatter.14
  32.4 1.9 dynamic-slice.29
  35.5 1.4 scatter.15
  38.0 9.1 %all-gather = f32[4,1,64]{2,1,0:T(1,128)S(1)} all-gather(f32[1,1,64]{2,1,0:T(1,128)S(1)} %convert_element_type.28), channel_id=2, replica_groups=mesh['brick'=128,'plane'=4] {'plane'}, dimensions={0}, use_global_device_ids=true | all-gather | bytes 1280 | tf_op jit(solution)/shard_map/all_gather | solution.py:140
  47.2 1.9 collective-permute-start.2
  49.1 3.9 collective-permute-start.3
  53.1 3.8 collective-permute-done.2
  56.9 6.0 collective-permute-done.3
  63.2 0.4 stack.12
  63.9 0.6 copy.46
  64.5 57.3 %while.14 = (s32[]{:T(128)}, f32[2,64,64]{1,2,0:T(8,128)S(1)}, s32[]{:T(128)}, s32[1752]{0:T(1024)S(1)}, f32[6,320,64]{2,0,1:T(8,128)S(1)}, /*index=5*/s32[]{:T(...) while((s32[]{:T(128)}, f32[2,64,64]{1,2,0:T(8,128)S(1)}, ...), condition=%wide.region_7.8_spmd, body=%wide.region_6.0_spmd.sunk | while | flops 72616448 | bytes 5868207 | solution.py:85
  64.6 0.7 dynamic-slice_compare_fusion.2
  65.3 1.0 gather_fusion.1
  66.7 0.4 slice_multiply_fusion.6
  67.1 1.0 gather_fusion
  68.1 0.3 select_bitcast_fusion.4
  68.5 0.4 slice_multiply_fusion.5
  68.9 23.9 %fusion.66 = f32[2,256,64]{2,0,1:T(2,128)S(1)} fusion(f32[256,64]{1,0:T(8,128)S(1)} %bitcast.106, f32[256,64]{1,0:T(8,128)S(1)} %bitcast.102, f32[256,64]{1,0:T(8,128)S(1)} %bitcast.107, f32[256,64]{1,0:T(8,128)S(1)} %bitcast.103, f32[256,64]{1,0:T(8,128)S(1)} %bitcast.108, f32[256,64]{1,0:T(8,128)S(1)} %bitcast.104, f32[256,64]{1,0:T(8,128)S(1)} %bitcast.105, ...), kind=kOutput, calls=%fused_computation.24.clone.3 | convolution fusion | flops 47185920 | bytes 1451008 | tf_op jit(solution)/shard_map/while/body/pij,cpj->cpi/dot_general | solution.py:64
  92.8 0.4 fusion.67
  93.2 0.7 dynamic-slice_compare_fusion.2
  94.0 1.0 gather_fusion.1
  95.0 0.3 select_bitcast_fusion.5
  95.4 0.4 slice_multiply_fusion.6
  95.8 1.0 gather_fusion
  96.8 0.3 select_bitcast_fusion.4
  97.2 0.4 slice_multiply_fusion.5
  97.6 23.9 %fusion.66 = f32[2,256,64]{2,0,1:T(2,128)S(1)} fusion(f32[256,64]{1,0:T(8,128)S(1)} %bitcast.106, f32[256,64]{1,0:T(8,128)S(1)} %bitcast.102, f32[256,64]{1,0:T(8,128)S(1)} %bitcast.107, f32[256,64]{1,0:T(8,128)S(1)} %bitcast.103, f32[256,64]{1,0:T(8,128)S(1)} %bitcast.108, f32[256,64]{1,0:T(8,128)S(1)} %bitcast.104, f32[256,64]{1,0:T(8,128)S(1)} %bitcast.105, ...), kind=kOutput, calls=%fused_computation.24.clone.3 | convolution fusion | flops 47185920 | bytes 1451008 | tf_op jit(solution)/shard_map/while/body/pij,cpj->cpi/dot_general | solution.py:64
  121.5 0.4 fusion.67
  122.0 0.6 fusion.44
  124.0 512.4 %all-reduce.2 = (f32[]{:T(128)}, f32[]{:T(128)}) all-reduce(f32[]{:T(128)S(6)} %add.169, f32[]{:T(128)} %divide_reduce_fusion), channel_id=1, replica_groups=mesh['brick'=128,'plane'=4] {'brick'}, use_global_device_ids=true, to_apply=%region_1.0 | all-reduce | flops 2 | bytes 16 | tf_op jit(solution)/shard_map/psum | solution.py:127
  636.4 11.1 %all-reduce.3 = (f32[]{:T(128)}, f32[]{:T(128)}) all-reduce(f32[]{:T(128)} %get-tuple-element.148, f32[]{:T(128)} %get-tuple-element.149), channel_id=1, replica_groups=mesh['brick'=128,'plane'=4] {'plane'}, use_global_device_ids=true, to_apply=%region_2.0 | all-reduce | flops 2 | bytes 16 | tf_op jit(solution)/shard_map/psum | solution.py:126
  648.9 12.0 %all_gather.6 = f32[4,2,64,64]{3,2,1,0:T(8,128)S(1)} all-gather(f32[1,2,64,64]{3,2,1,0:T(8,128)S(1)} %pad_maximum_fusion.3), channel_id=1, replica_groups=mesh['brick'=128,'plane'=4] {'plane'}, dimensions={0}, use_global_device_ids=true | all-gather | bytes 163840 | tf_op jit(solution)/shard_map/all_gather | solution.py:139
  662.1 0.6 subtract_add_fusion
  662.7 0.6 subtract_divide_fusion
  (72 shorter events, 3.8 us)
Async XLA Ops:
  0.6 37.3 %copy-start = (f32[1,1,4096]{2,1,0:T(1,128)S(1)}, f32[1,1,4096]{2,1,0:T(1,128)}, u32[]{:S(2)}) copy-start(f32[1,1,4096]{2,1,0:T(1,128)} %param.23) | copy-start | bytes 49156
  0.6 37.2 %copy-start.3 = (s32[1,1,1496]{2,1,0:T(1,128)S(1)}, s32[1,1,1496]{2,1,0:T(1,128)}, u32[]{:S(2)}) copy-start(s32[1,1,1496]{2,1,0:T(1,128)} %param.28) | copy-start | bytes 17956
  0.7 37.2 %copy-start.4 = (s32[1,1,1496]{2,1,0:T(1,128)S(1)}, s32[1,1,1496]{2,1,0:T(1,128)}, u32[]{:S(2)}) copy-start(s32[1,1,1496]{2,1,0:T(1,128)} %param.27) | copy-start | bytes 17956
  0.7 37.3 %copy-start.5 = (s32[1,1,64]{2,1,0:T(1,128)S(1)}, s32[1,1,64]{2,1,0:T(1,128)}, u32[]{:S(2)}) copy-start(s32[1,1,64]{2,1,0:T(1,128)} %param.30) | copy-start | bytes 772
  3.2 43.9 %collective-permute-start = (f32[1,1,6,4096]{3,2,1,0:T(8,128)S(1)}, f32[1,1,6,4096]{3,2,1,0:T(8,128)S(1)}, u32[]{:S(2)}, u32[]{:S(2)}) collective-permute-start(f32[1,1,6,4096]{3,2,1,0:T(8,128)S(1)} %fusion.37), channel_id=1, source_target_pairs={{0,4},{4,8},{8,12},{12,16},{16,20},{20,24},{24,28},{28,32},{32,36}... | collective-permute-start | bytes 294920 | tf_op jit(solution)/shard_map/ppermute | solution.py:22
  5.2 42.0 %collective-permute-start.1 = (f32[1,1,6,4096]{3,2,1,0:T(8,128)S(1)}, f32[1,1,6,4096]{3,2,1,0:T(8,128)S(1)}, u32[]{:S(2)}, u32[]{:S(2)}) collective-permute-start(f32[1,1,6,4096]{3,2,1,0:T(8,128)S(1)} %fusion.37), channel_id=1, source_target_pairs={{4,0},{8,4},{12,8},{16,12},{20,16},{24,20},{28,24},{32,28},{36,32}... | collective-permute-start | bytes 294920 | tf_op jit(solution)/shard_map/ppermute | solution.py:25
  47.2 9.7 %collective-permute-start.2 = (f32[3,1,6,4096]{3,2,1,0:T(8,128)S(1)}, f32[3,1,6,4096]{3,2,1,0:T(8,128)S(1)}, u32[]{:S(2)}, u32[]{:S(2)}) collective-permute-start(f32[3,1,6,4096]{3,2,1,0:T(8,128)S(1)} %pad_maximum_fusion), channel_id=1, source_target_pairs={{0,1},{1,2},{2,3},{3,0},{4,5},{5,6},{6,7},{7,4},{8,9},{9,10},{10,1... | collective-permute-start | bytes 884744 | tf_op jit(solution)/shard_map/ppermute | solution.py:22
  49.1 13.8 %collective-permute-start.3 = (f32[3,1,6,4096]{3,2,1,0:T(8,128)S(1)}, f32[3,1,6,4096]{3,2,1,0:T(8,128)S(1)}, u32[]{:S(2)}, u32[]{:S(2)}) collective-permute-start(f32[3,1,6,4096]{3,2,1,0:T(8,128)S(1)} %pad_maximum_fusion), channel_id=1, source_target_pairs={{1,0},{2,1},{3,2},{0,3},{5,4},{6,5},{7,6},{4,7},{9,8},{10,9},{11,1... | collective-permute-start | bytes 884744 | tf_op jit(solution)/shard_map/ppermute | solution.py:25
  121.9 540.2 %copy-start.2 = (f32[1,1,4096]{2,1,0:T(1,128)S(1)}, f32[1,1,4096]{2,1,0:T(1,128)}, u32[]{:S(2)}) copy-start(f32[1,1,4096]{2,1,0:T(1,128)} %param.24) | copy-start | bytes 49156
  662.1 1.3 copy-start.1
